TPU v7x, 32 devices: a whole 2x2x4 slice. The times are simulated.
32 devices in a mesh: groups: 2 (over x), rollout: 2 (over core), tensor: 8 (over z, y).
Axes of the slice: x: 2, y: 2, z: 4, core: 2. Of those that a mesh axis runs over, the one named last changes fastest.
Arguments:
- hidden_in: bfloat16 [128, 8192], P(('groups', 'tensor'), 'rollout'), parts along dimension 0, may hold values from -6 to 6
- norm_gain: float32 [8192], P('rollout'), may hold values from 0.1 to 1.9
- w_gate: bfloat16 [8192, 29568], P('rollout', 'tensor'), may hold values from -0.0625 to 0.0625
- w_up: bfloat16 [8192, 29568], P('rollout', 'tensor'), may hold values from -0.0625 to 0.0625
- w_down: bfloat16 [29568, 8192], P('tensor', 'rollout'), may hold values from -0.03125 to 0.03125
- width_factors: bfloat16 [6, 8192, 64], P('groups', ('rollout', 'tensor')), parts along dimension 0, may hold values from -0.0625 to 0.0625
- unit_factors: bfloat16 [6, 29568, 64], P('groups', ('rollout', 'tensor')), parts along dimension 0, may hold values from -1.5 to 1.5
- slot_block: int32 [32], P('groups'), parts along dimension 0, may hold values from 0 to 15, each once
Outputs:
- hidden_out: bfloat16 [128, 8192], P(('groups', 'tensor'), 'rollout'), parts along dimension 0
There are 2 independent parts, one for each index of `groups`. A program takes and returns all parts, laid end to end along the dimension named above; an argument that names none is the same for every part. Nothing has to cross between parts.
Inputs may be any that keep to these rules, and one draw needn't show every extreme that they name: `slot_block`: each block number appears exactly once.
All inputs are finite; a program needn't handle non-finite values.
Results may differ from a plain program's by a relative error of at most 0.008.
Values may be sent and summed in bfloat16 or wider, within the bound.
A program may use at most 256 MiB of HBM per device.

v0:
```python
import jax
import jax.numpy as jnp
from jax import lax
from jax.sharding import PartitionSpec as P

D = 8192


def on_device(hidden_in, norm_gain, w_gate, w_up, w_down, width_factors, unit_factors, slot_block):
    n_replica = lax.axis_size("rollout")
    n_tensor = lax.axis_size("tensor")
    tensor_idx = lax.axis_index("tensor")
    block = unit_factors.shape[1]
    rank_cols = unit_factors.shape[2]
    units = w_gate.shape[1]
    wanted = tensor_idx * n_replica + jnp.arange(n_replica, dtype=jnp.int32)
    width_half = lax.all_gather(width_factors, "tensor", axis=1, tiled=True)
    pieces = lax.all_gather(unit_factors, ("rollout", "tensor"), axis=1, tiled=True)
    pieces = pieces.reshape(3, n_replica * n_tensor, block, rank_cols)
    select = (slot_block[None, :] == wanted[:, None]).astype(jnp.bfloat16)
    mine = jnp.einsum("js,ksbr->kjbr", select, pieces, preferred_element_type=jnp.float32).astype(
        jnp.bfloat16
    )
    mine = mine.reshape(3, n_replica * block, rank_cols)
    gate_merged = (
        w_gate + 0.5 * jnp.dot(width_half[0], mine[0].T, preferred_element_type=jnp.float32)
    ).astype(jnp.bfloat16)
    up_merged = (
        w_up + 0.5 * jnp.dot(width_half[1], mine[1].T, preferred_element_type=jnp.float32)
    ).astype(jnp.bfloat16)
    down_merged = (
        w_down + 0.5 * jnp.dot(mine[2], width_half[2].T, preferred_element_type=jnp.float32)
    ).astype(jnp.bfloat16)
    wide = hidden_in.astype(jnp.float32)
    squares = lax.psum(jnp.sum(wide * wide, axis=1, keepdims=True), "rollout")
    power = squares / D
    normed = (wide * lax.rsqrt(power + 1e-06) * norm_gain[None, :]).astype(jnp.bfloat16)
    piece = lax.all_gather(normed, "tensor", axis=0, tiled=True)
    gate = jnp.dot(piece, gate_merged, preferred_element_type=jnp.float32)
    upper = jnp.dot(piece, up_merged, preferred_element_type=jnp.float32)
    partial_both = jnp.concatenate([gate, upper], axis=1)
    both = lax.psum(partial_both, "rollout")
    activated = (jax.nn.silu(both[:, :units]) * both[:, units:]).astype(jnp.bfloat16)
    terms = jnp.dot(activated, down_merged, preferred_element_type=jnp.float32)
    mixed = lax.psum_scatter(terms, "tensor", scatter_dimension=0, tiled=True)
    return (wide + mixed).astype(jnp.bfloat16)


def solution(mesh):
    in_specs = (
        P(("groups", "tensor"), "rollout"),
        P("rollout"),
        P("rollout", "tensor"),
        P("rollout", "tensor"),
        P("tensor", "rollout"),
        P("groups", ("rollout", "tensor"), None),
        P("groups", ("rollout", "tensor"), None),
        P("groups"),
    )
    out_specs = P(("groups", "tensor"), "rollout")
    return jax.shard_map(
        on_device, mesh=mesh, in_specs=in_specs, out_specs=out_specs, check_vma=False
    )
```

profile of v0, /device:TPU:0, one launch (start us, length us, event | category | flops | bytes accessed | tf_op | source)
XLA Modules:
  0.0 382.3 jit_solution(5265986821756409067)
XLA Ops:
  6.5 0.0 copy-start.1
  6.5 0.0 all-gather.3.cloned.1.call-start
  6.5 3.6 copy.9
  10.2 0.0 all-gather.3.cloned.1.call-update
  10.2 0.0 all-gather.5.cloned.1.call-start
  10.2 0.7 all-gather.5.cloned.1.call-update
  10.9 0.0 all-reduce.2.cloned.1.call-start
  11.0 1.0 fusion.9
  12.0 2.6 psum.14
  14.6 0.9 fusion.11
  15.5 34.6 %all_gather.9 = bf16[64,4096]{1,0:T(8,128)(2,1)S(1)} all-gather(bf16[8,4096]{1,0:T(8,128)(2,1)S(1)} %fusion.11), channel_id=1, replica_groups=mesh['groups'=2,'rollout'=2,'tensor'=8] {'tensor'}, dimensions={0}, use_global_device_ids=true | all-gather | bytes 589824 | tf_op jit(solution)/shard_map/all_gather | solution.py:38
  50.1 124.8 %all-gather.3.cloned.1.call-done = bf16[3,29568,64]{2,0,1:T(4,128)(2,1)} async-done(((bf16[3,1848,64]{2,0,1:T(4,128)(2,1)}), bf16[3,29568,64]{2,0,1:T(4,128)(2,1)}) %all-gather.3.cloned.1.call-update) | async-done | bytes 11354128 | tf_op jit(solution)/shard_map/all_gather | solution.py:18
  174.9 31.2 %copy.12 = bf16[3,16,1848,64]{2,1,3,0:T(8,128)(2,1)} copy(bf16[3,16,1848,64]{3,0,2,1:T(4,128)(2,1)} %bitcast.47) | data formatting | bytes 22708224 | tf_op jit(solution)/shard_map/reshape | solution.py:19
  206.1 0.0 copy-done.1
  206.1 6.2 %fusion.5 = bf16[3,2,1848,64]{2,1,3,0:T(2,128)(2,1)S(1)} fusion(bf16[3,16,1848,64]{2,1,3,0:T(8,128)(2,1)} %copy.12, s32[16]{0:T(128)S(1)} %copy-done.1, s32[2]{0:T(128)S(1)} %iota_add_fusion), kind=kOutput, calls=%fused_computation.9 | convolution fusion | flops 23417888 | bytes 12773448 | tf_op jit(solution)/shard_map/js,ksbr->kjbr/dot_general | solution.py:21
  212.2 1.0 fusion.21
  213.3 0.3 squeeze.18
  213.6 0.3 squeeze.20
  214.0 8.5 %all-gather.5.cloned.1.call-done = bf16[3,4096,64]{1,2,0:T(8,128)(2,1)} async-done(((bf16[3,512,64]{1,2,0:T(8,128)(2,1)}), bf16[3,4096,64]{1,2,0:T(8,128)(2,1)}) %all-gather.5.cloned.1.call-update) | async-done | bytes 1572880 | tf_op jit(solution)/shard_map/all_gather | solution.py:17
  222.5 23.1 %fusion.2 = f32[64,3696]{1,0:T(8,128)S(1)} fusion(bf16[64,4096]{1,0:T(8,128)(2,1)S(1)} %all_gather.9, bf16[4096,3696]{0,1:T(8,128)(2,1)} %param.10, bf16[3696,64]{0,1:T(8,128)(2,1)S(1)} %squeeze.18, bf16[3,4096,64]{1,2,0:T(8,128)(2,1)} %all-gather.5.cloned.1.call-done), kind=kOutput, calls=%fused_computation.5 | convolution fusion | flops 3936092160 | bytes 32745472 | tf_op jit(solution)/shard_map/dot_general | solution.py:39
  245.6 23.3 %fusion.3 = f32[64,3696]{1,0:T(8,128)S(1)} fusion(bf16[64,4096]{1,0:T(8,128)(2,1)S(1)} %all_gather.9, bf16[4096,3696]{0,1:T(8,128)(2,1)} %param.11, bf16[3696,64]{0,1:T(8,128)(2,1)S(1)} %squeeze.20, bf16[3,4096,64]{1,2,0:T(8,128)(2,1)} %all-gather.5.cloned.1.call-done), kind=kOutput, calls=%fused_computation.6 | convolution fusion | flops 3936092160 | bytes 32745472 | tf_op jit(solution)/shard_map/dot_general | solution.py:40
  268.9 1.6 pad_maximum_fusion
  270.5 0.0 all-reduce.2.cloned.1.call-update
  270.5 0.0 reduce-scatter.2.cloned.1.call-start
  270.6 0.3 squeeze.22
  270.9 0.0 copy-start
  270.9 18.8 %all-reduce.2.cloned.1.call-done = f32[64,7392]{1,0:T(8,128)} async-done(((f32[64,7392]{1,0:T(8,128)}), f32[64,7392]{1,0:T(8,128)}) %all-reduce.2.cloned.1.call-update) | async-done | bytes 1892368 | tf_op jit(solution)/shard_map/psum | solution.py:42
  289.8 19.6 %fusion.4 = f32[64,4096]{1,0:T(8,128)} fusion(bf16[3696,4096]{1,0:T(8,128)(2,1)} %param.12, bf16[3696,64]{0,1:T(8,128)(2,1)S(1)} %squeeze.22, bf16[3,4096,64]{1,2,0:T(8,128)(2,1)} %all-gather.5.cloned.1.call-done, f32[64,7392]{1,0:T(8,128)} %all-reduce.2.cloned.1.call-done), kind=kOutput, calls=%fused_computation.7 | convolution fusion | flops 3937511424 | bytes 34224128 | tf_op jit(solution)/shard_map/dot_general | solution.py:44
  309.4 0.0 reduce-scatter.2.cloned.1.call-update
  309.4 64.8 %reduce-scatter.2.cloned.1.call-done = f32[8,4096]{1,0:T(8,128)} async-done(((f32[64,4096]{1,0:T(8,128)}), f32[8,4096]{1,0:T(8,128)}) %reduce-scatter.2.cloned.1.call-update) | async-done | bytes 131088 | tf_op jit(solution)/shard_map/reduce_scatter | solution.py:45
  374.2 0.0 copy-done
  374.2 1.5 fusion.12
  (2 shorter events, 0.0 us)
Async XLA Ops:
  6.5 199.5 %copy-start.1 = (s32[16]{0:T(128)S(1)}, s32[16]{0:T(128)}, u32[]{:S(2)}) copy-start(s32[16]{0:T(128)} %param.15) | copy-start | bytes 196
  6.5 168.3 %all-gather.3.cloned.1.call-start = ((), (), s32[]{:S(2)}) async-start(), calls=%async_computation.1 | async-start | bytes 32169984 | tf_op jit(solution)/shard_map/all_gather | solution.py:18
  10.2 212.3 %all-gather.5.cloned.1.call-start = ((), (), s32[]{:S(2)}) async-start(), calls=%async_computation.2 | async-start | bytes 1769472 | tf_op jit(solution)/shard_map/all_gather | solution.py:17
  10.9 278.8 %all-reduce.2.cloned.1.call-start = ((), (), s32[]{:S(2)}) async-start(), calls=%async_computation.3 | async-start | bytes 3801088 | tf_op jit(solution)/shard_map/psum | solution.py:42
  270.5 103.7 %reduce-scatter.2.cloned.1.call-start = ((), (), s32[]{:S(2)}) async-start(), calls=%async_computation.4 | async-start | bytes 1179648 | tf_op jit(solution)/shard_map/reduce_scatter | solution.py:45
  270.9 103.3 %copy-start = (bf16[8,4096]{1,0:T(8,128)(2,1)S(1)}, bf16[8,4096]{1,0:T(8,128)(2,1)}, u32[]{:S(2)}) copy-start(bf16[8,4096]{1,0:T(8,128)(2,1)} %param.8) | copy-start | bytes 196612
Sparse Core Ops, SparseCore 0:
  10.3 164.5 all-gather.2
  176.9 45.5 all-gather.4
  270.6 19.0 all-reduce.1
  309.5 64.6 reduce-scatter.1
where the time goes:
time: 383 us; the launch traced here: 382 us
  waiting for transfers between devices  218 us (57%)
  matrix products  72.2 us (19%)
  blocking collectives  37.2 us (10%)
  local copies, waits for them, and re-layouts  36.9 us (10%)
  between operations  13.2 us (3%)
  other arithmetic  5.05 us (1%)
    all_gather x1, waiting for transfers between devices, on_device(): lax.all_gather(unit_factors, ('rollout', 'tensor'), axis=1, tiled=True)  125 us
    reduce_scatter x1, waiting for transfers between devices, on_device(): mixed = lax.psum_scatter(terms, 'tensor', scatter_dimension=0, tiled=True)  64.8 us
    all_gather x1, blocking collectives, on_device(): piece = lax.all_gather(normed, 'tensor', axis=0, tiled=True)  34.6 us
    reshape x1, local copies, waits for them, and re-layouts, on_device(): pieces = pieces.reshape(3, n_replica * n_tensor, block, rank_cols)  31.2 us
    dot_general x1, matrix products, on_device(): upper = jnp.dot(piece, up_merged, preferred_element_type=jnp.float32)  23.3 us
    dot_general x1, matrix products, on_device(): gate = jnp.dot(piece, gate_merged, preferred_element_type=jnp.float32)  23.1 us
    dot_general x1, matrix products, on_device(): terms = jnp.dot(activated, down_merged, preferred_element_type=jnp.float32)  19.6 us
    psum x1, waiting for transfers between devices, on_device(): both = lax.psum(partial_both, 'rollout')  18.8 us
  transfers between devices with their start and end apart: 4, of which 4 were waited for; matrix products, arithmetic and copies ran while one was open for 11% of the time, Pallas kernels for 0%

commit v1 on v0

v1 whole, which is shorter than its diff:
```python
import jax
import jax.numpy as jnp
from jax import lax
from jax.sharding import PartitionSpec as P

D = 8192


def on_device(hidden_in, norm_gain, w_gate, w_up, w_down, width_factors, unit_factors, slot_block):
    n_replica = lax.axis_size("rollout")
    n_tensor = lax.axis_size("tensor")
    n = n_replica * n_tensor
    block = unit_factors.shape[1]
    rank = unit_factors.shape[2]
    units = w_gate.shape[1]
    f32 = jnp.float32
    flat = jnp.swapaxes(unit_factors, 1, 2).reshape(3 * rank, block)
    per = -(-3 * rank // n)
    flat = jnp.pad(flat, ((0, per * n - 3 * rank), (0, 0))).reshape(n, per, block)
    every = lax.all_to_all(flat, ("rollout", "tensor"), 0, 0, tiled=True)
    dest = jnp.arange(n, dtype=jnp.int32)
    wanted = (dest % n_tensor) * n_replica + dest // n_tensor
    select = jnp.argmax(slot_block[None, :] == wanted[:, None], axis=1)
    sorted_ = jnp.take(every, select, axis=0)
    own = lax.all_to_all(sorted_, ("rollout", "tensor"), 0, 0, tiled=True)
    own = own.reshape(n * per, block)[: 3 * rank]
    both_b = lax.all_gather(own, "rollout", axis=1, tiled=True).reshape(3, rank, units)

    rows = lax.all_gather(hidden_in, "tensor", axis=0, tiled=True)
    width_half = lax.all_gather(width_factors, "tensor", axis=1, tiled=True)
    wide = rows.astype(f32)
    squares = lax.psum(jnp.sum(wide * wide, axis=1, keepdims=True), "rollout")
    scaled = (wide * norm_gain[None, :]).astype(jnp.bfloat16)
    xa = [
        (0.5 * jnp.dot(scaled, width_half[k], preferred_element_type=f32)).astype(jnp.bfloat16)
        for k in range(2)
    ]
    gate = jnp.dot(scaled, w_gate, preferred_element_type=f32)
    upper = jnp.dot(scaled, w_up, preferred_element_type=f32)
    gate = gate + jnp.dot(xa[0], both_b[0], preferred_element_type=f32)
    upper = upper + jnp.dot(xa[1], both_b[1], preferred_element_type=f32)
    gate = lax.psum(gate, "rollout")
    upper = lax.psum(upper, "rollout")
    inv = lax.rsqrt(squares / D + 1e-06)
    activated = (jax.nn.silu(gate * inv) * (upper * inv)).astype(jnp.bfloat16)
    ab = lax.dot_general(activated, both_b[2], (((1,), (1,)), ((), ())), preferred_element_type=f32)
    terms = jnp.dot(activated, w_down, preferred_element_type=f32)
    terms = terms + 0.5 * lax.dot_general(
        ab.astype(jnp.bfloat16), width_half[2], (((1,), (1,)), ((), ())), preferred_element_type=f32
    )
    mixed = lax.psum_scatter(terms, "tensor", scatter_dimension=0, tiled=True)
    return (hidden_in.astype(f32) + mixed).astype(jnp.bfloat16)


def solution(mesh):
    in_specs = (
        P(("groups", "tensor"), "rollout"),
        P("rollout"),
        P("rollout", "tensor"),
        P("rollout", "tensor"),
        P("tensor", "rollout"),
        P("groups", ("rollout", "tensor"), None),
        P("groups", ("rollout", "tensor"), None),
        P("groups"),
    )
    out_specs = P(("groups", "tensor"), "rollout")
    return jax.shard_map(
        on_device, mesh=mesh, in_specs=in_specs, out_specs=out_specs, check_vma=False
    )
```

time: 383 us -> 255 us (0.67)
  waiting for transfers between devices: 218 us -> 106 us
  local copies, waits for them, and re-layouts: 36.9 us -> 8.12 us
  blocking collectives: 37.2 us -> 62.7 us
  matrix products: 72.2 us -> 52.4 us
  starting transfers between devices: 0.12 us -> 7.55 us
    all_gather x1, waiting for transfers between devices: 125 us -> 0.01 us  [on_device(): lax.all_gather(own, 'rollout', axis=1, tiled=True).reshape(3, rank, units)]
    all_to_all x0 -> x1, blocking collectives: none -> 28.3 us  [on_device(): own = lax.all_to_all(sorted_, ('rollout', 'tensor'), 0, 0, tiled=True)]
    reshape x1 -> x2, local copies, waits for them, and re-layouts: 31.2 us -> 3.48 us  [the longest x1 2.22 us: on_device(): jnp.pad(flat, ((0, per * n - 3 * rank), (0, 0))).reshape(n, per, block)]
    all_to_all x0 -> x1, waiting for transfers between devices: none -> 24.3 us  [on_device(): every = lax.all_to_all(flat, ('rollout', 'tensor'), 0, 0, tiled=True)]
    dot_general x4 -> x6, matrix products: 72.2 us -> 52.4 us  [the longest x1 15.6 us: on_device(): gate = jnp.dot(scaled, w_gate, preferred_element_type=f32)]
    all_gather x1, waiting for transfers between devices: 8.52 us -> 0.02 us  [on_device(): width_half = lax.all_gather(width_factors, 'tensor', axis=1, tiled=True)]
    all_to_all x0 -> x1, starting transfers between devices: none -> 7.39 us  [on_device(): every = lax.all_to_all(flat, ('rollout', 'tensor'), 0, 0, tiled=True)]
  transfers between devices with their start and end apart: 4 -> 5, of which waited for: 4 -> 3; matrix products, arithmetic and copies ran while one was open for 11% -> 14% of each run, Pallas kernels for 0% -> 0%
where the time goes in v1:
time: 255 us
  waiting for transfers between devices  106 us (42%)
  blocking collectives  62.7 us (25%)
  matrix products  52.4 us (21%)
  between operations  13.2 us (5%)
  local copies, waits for them, and re-layouts  8.12 us (3%)
  starting transfers between devices  7.55 us (3%)
  other arithmetic  4.47 us (2%)
    reduce_scatter x1, waiting for transfers between devices, on_device(): mixed = lax.psum_scatter(terms, 'tensor', scatter_dimension=0, tiled=True)  65.1 us
    all_gather x1, blocking collectives, on_device(): rows = lax.all_gather(hidden_in, 'tensor', axis=0, tiled=True)  31.8 us
    all_to_all x1, blocking collectives, on_device(): own = lax.all_to_all(sorted_, ('rollout', 'tensor'), 0, 0, tiled=True)  28.3 us
    all_to_all x1, waiting for transfers between devices, on_device(): every = lax.all_to_all(flat, ('rollout', 'tensor'), 0, 0, tiled=True)  24.3 us
    psum x1, waiting for transfers between devices, on_device(): upper = lax.psum(upper, 'rollout')  15.9 us
    dot_general x1, matrix products, on_device(): gate = jnp.dot(scaled, w_gate, preferred_element_type=f32)  15.6 us
    dot_general x1, matrix products, on_device(): upper = jnp.dot(scaled, w_up, preferred_element_type=f32)  15.6 us
    dot_general x1, matrix products, on_device(): terms = jnp.dot(activated, w_down, preferred_element_type=f32)  13.7 us
  transfers between devices with their start and end apart: 5, of which 3 were waited for; matrix products, arithmetic and copies ran while one was open for 14% of the time, Pallas kernels for 0%

profile of v1, /device:TPU:0, one launch (start us, length us, event | category | flops | bytes accessed | tf_op | source)
XLA Modules:
  0.0 254.7 jit_solution(16169316417375113845)
XLA Ops:
  6.5 0.0 copy-start.3
  6.5 2.2 reshape.44
  8.8 7.4 %all-to-all-start = ((bf16[16,12,1848]{2,1,0:T(8,128)(2,1)}), bf16[16,12,1848]{2,1,0:T(8,128)(2,1)S(1)}, u32[]{:S(2)}, u32[]{:S(2)}) async-start(bf16[16,12,1848]{2,1,0:T(8,128)(2,1)} %reshape.44), calls=%async_computation | async-start | bytes 1966080 | tf_op jit(solution)/shard_map/all_to_all | solution.py:20
  16.2 0.0 all-gather.6.cloned.1.call-start
  16.2 0.0 copy-done.3
  16.2 0.7 iota_reduce_fusion
  16.9 24.3 %all-to-all-done = bf16[16,12,1848]{2,1,0:T(8,128)(2,1)S(1)} async-done(((bf16[16,12,1848]{2,1,0:T(8,128)(2,1)}), bf16[16,12,1848]{2,1,0:T(8,128)(2,1)S(1)}, u32[]{:S(2)}, u32[]{:S(2)}) %all-to-all-start) | async-done | bytes 709664 | tf_op jit(solution)/shard_map/all_to_all | solution.py:20
  41.3 0.7 gather_fusion
  42.0 0.2 broadcast_select_fusion
  42.2 28.3 %all_to_all.10 = bf16[16,12,1848]{2,1,0:T(8,128)(2,1)S(1)} all-to-all(bf16[16,12,1848]{2,1,0:T(8,128)(2,1)S(1)} %broadcast_select_fusion), channel_id=1, replica_groups=mesh['groups'=2,'rollout'=2,'tensor'=8] {'rollout','tensor'}, dimensions={0} | all-to-all | bytes 1419264 | tf_op jit(solution)/shard_map/all_to_all | solution.py:25
  70.5 0.0 copy-start.2
  70.5 0.0 copy-start.1
  70.5 1.3 reshape.45
  71.7 0.0 all-gather.6.cloned.1.call-update
  71.7 0.0 all-gather.4.cloned.1.call-start
  71.8 0.7 all-gather.4.cloned.1.call-update
  72.5 0.0 all-reduce.3.cloned.1.call-start
  72.5 0.0 copy-done.2
  72.5 31.8 %all_gather.9 = bf16[64,4096]{1,0:T(8,128)(2,1)S(1)} all-gather(bf16[8,4096]{1,0:T(8,128)(2,1)S(1)} %copy-done.2), channel_id=1, replica_groups=mesh['groups'=2,'rollout'=2,'tensor'=8] {'tensor'}, dimensions={0}, use_global_device_ids=true | all-gather | bytes 589824 | tf_op jit(solution)/shard_map/all_gather | solution.py:29
  104.4 0.0 copy-done.1
  104.4 15.6 %fusion.10 = f32[64,3696]{1,0:T(8,128)} fusion(bf16[4096,3696]{0,1:T(8,128)(2,1)} %param.11, bf16[64,4096]{1,0:T(8,128)(2,1)S(1)} %all_gather.9, f32[4096]{0:T(1024)S(1)} %copy-done.1), kind=kOutput, calls=%fused_computation.22 | convolution fusion | flops 1938554880 | bytes 31764480 | tf_op jit(solution)/shard_map/dot_general | solution.py:39
  119.9 15.6 %fusion.14 = f32[64,3696]{1,0:T(8,128)} fusion(bf16[4096,3696]{0,1:T(8,128)(2,1)} %param.10, bf16[64,4096]{1,0:T(8,128)(2,1)S(1)} %all_gather.9, f32[4096]{0:T(1024)S(1)} %copy-done.1), kind=kOutput, calls=%fused_computation.23 | convolution fusion | flops 1938554880 | bytes 31764480 | tf_op jit(solution)/shard_map/dot_general | solution.py:38
  135.5 0.0 all-gather.6.cloned.1.call-done
  135.5 2.9 %copy.11 = bf16[2,1848,192]{1,0,2:T(2,128)(2,1)S(1)} copy(bf16[2,1848,192]{1,2,0:T(8,128)(2,1)} %all-gather.6.cloned.1.call-done) | data formatting | bytes 2838528 | tf_op jit(solution)/shard_map/all_gather | solution.py:27
  138.4 1.1 reshape.56
  139.5 0.0 all-gather.4.cloned.1.call-done
  139.5 0.0 copy-start
  139.5 3.1 %convolution_add_fusion = f32[64,3696]{1,0:T(8,128)} fusion(f32[64,3696]{1,0:T(8,128)} %fusion.10, bf16[3,4096,64]{1,2,0:T(8,128)(2,1)} %all-gather.4.cloned.1.call-done, bf16[192,3696]{1,0:T(8,128)(2,1)S(1)} %bitcast.26, bf16[64,4096]{1,0:T(8,128)(2,1)S(1)} %all_gather.9, f32[4096]{0:T(1024)S(1)} %copy-done.1), kind=kOutput, calls=%fused_computation.1 | convolution fusion | flops 64863232 | bytes 3436544 | tf_op jit(solution)/shard_map/dot_general | solution.py:41
  142.6 0.0 copy-done
  142.6 2.7 %convolution_add_fusion.1 = f32[64,3696]{1,0:T(8,128)} fusion(f32[64,3696]{1,0:T(8,128)S(1)} %copy-done, bf16[3,4096,64]{1,2,0:T(8,128)(2,1)} %all-gather.4.cloned.1.call-done, bf16[192,3696]{1,0:T(8,128)(2,1)S(1)} %bitcast.27, bf16[64,4096]{1,0:T(8,128)(2,1)S(1)} %all_gather.9, f32[4096]{0:T(1024)S(1)} %copy-done.1), kind=kOutput, calls=%fused_computation.2 | convolution fusion | flops 64863232 | bytes 3436544 | tf_op jit(solution)/shard_map/dot_general | solution.py:40
  145.4 0.0 all-reduce.3.cloned.1.call-update
  145.4 0.0 reduce-scatter.2.cloned.1.call-start
  145.4 0.2 fusion.3
  145.6 2.6 %psum.22 = f32[64,1]{0,1:T(1,128)S(1)} all-reduce(f32[64,1]{0,1:T(1,128)S(1)} %bitcast.31), channel_id=1, replica_groups=mesh['groups'=2,'rollout'=2,'tensor'=8] {'rollout'}, use_global_device_ids=true, to_apply=%region_3.4 | all-reduce | flops 64 | bytes 512 | tf_op jit(solution)/shard_map/psum | solution.py:32
  148.3 15.9 %all-reduce.3.cloned.1.call-done = (f32[64,3696]{1,0:T(8,128)}, f32[64,3696]{1,0:T(8,128)}) async-done(((f32[64,3696]{1,0:T(8,128)}, f32[64,3696]{1,0:T(8,128)}), (f32[64,3696]{1,0:T(8,128)}, f32[64,3696]{1,0:T(8,128)})) %all-reduce.3.cloned.1.call-update) | async-done | bytes 1892368 | tf_op jit(solution)/shard_map/psum | solution.py:43
  164.2 1.8 multiply_convert_fusion
  166.0 1.8 convolution_multiply_fusion
  167.8 13.7 %convolution_add_fusion.2 = f32[64,4096]{1,0:T(8,128)} fusion(f32[64,4096]{1,0:T(8,128)S(1)} %convolution_multiply_fusion, bf16[64,3696]{1,0:T(8,128)(2,1)S(1)} %multiply_convert_fusion, bf16[3696,4096]{1,0:T(8,128)(2,1)} %param.12), kind=kOutput, calls=%fused_computation.4 | convolution fusion | flops 1938030592 | bytes 32847872 | tf_op jit(solution)/shard_map/dot_general | solution.py:47
  181.4 0.0 reduce-scatter.2.cloned.1.call-update
  181.5 65.1 %reduce-scatter.2.cloned.1.call-done = f32[8,4096]{1,0:T(8,128)} async-done(((f32[64,4096]{1,0:T(8,128)}), f32[8,4096]{1,0:T(8,128)}) %reduce-scatter.2.cloned.1.call-update) | async-done | bytes 131088 | tf_op jit(solution)/shard_map/reduce_scatter | solution.py:51
  246.6 1.5 add_convert_fusion
  (5 shorter events, 0.0 us)
Async XLA Ops:
  6.5 9.7 %copy-start.3 = (s32[16]{0:T(128)S(1)}, s32[16]{0:T(128)}, u32[]{:S(2)}) copy-start(s32[16]{0:T(128)} %param.15) | copy-start | bytes 196
  8.8 32.5 %all-to-all-start = ((bf16[16,12,1848]{2,1,0:T(8,128)(2,1)}), bf16[16,12,1848]{2,1,0:T(8,128)(2,1)S(1)}, u32[]{:S(2)}, u32[]{:S(2)}) async-start(bf16[16,12,1848]{2,1,0:T(8,128)(2,1)} %reshape.44), calls=%async_computation | async-start | bytes 1966080 | tf_op jit(solution)/shard_map/all_to_all | solution.py:20
  16.2 119.4 %all-gather.6.cloned.1.call-start = ((), (), s32[]{:S(2)}) async-start(), calls=%async_computation.5 | async-start | bytes 2211840 | tf_op jit(solution)/shard_map/all_gather | solution.py:27
  70.5 2.1 copy-start.2
  70.5 33.9 %copy-start.1 = (f32[4096]{0:T(1024)S(1)}, f32[4096]{0:T(1024)}, u32[]{:S(2)}) copy-start(f32[4096]{0:T(1024)} %param.9) | copy-start | bytes 49156
  71.7 67.8 %all-gather.4.cloned.1.call-start = ((), (), s32[]{:S(2)}) async-start(), calls=%async_computation.3 | async-start | bytes 1769472 | tf_op jit(solution)/shard_map/all_gather | solution.py:30
  72.5 91.7 %all-reduce.3.cloned.1.call-start = ((), (), s32[]{:S(2)}) async-start(), calls=%async_computation.6 | async-start | bytes 3801088 | tf_op jit(solution)/shard_map/psum | solution.py:43
  139.5 3.1 %copy-start = (f32[64,3696]{1,0:T(8,128)S(1)}, f32[64,3696]{1,0:T(8,128)}, u32[]{:S(2)}) copy-start(f32[64,3696]{1,0:T(8,128)} %fusion.14) | copy-start | bytes 2838532
  145.4 101.2 %reduce-scatter.2.cloned.1.call-start = ((), (), s32[]{:S(2)}) async-start(), calls=%async_computation.4 | async-start | bytes 1179648 | tf_op jit(solution)/shard_map/reduce_scatter | solution.py:51
Sparse Core Ops, SparseCore 0:
  71.9 7.4 all-gather.5
  81.4 47.6 all-gather.3
  145.5 18.6 all-reduce.2
  181.6 64.9 reduce-scatter.1

commit v2 on v1

--- a/solution.py
+++ b/solution.py
@@ -1,12 +1,14 @@
 import jax
 import jax.numpy as jnp
 from jax import lax
+from jax.experimental import pallas as pl
+from jax.experimental.pallas import tpu as pltpu
 from jax.sharding import PartitionSpec as P
 
 D = 8192
 
 
-def on_device(hidden_in, norm_gain, w_gate, w_up, w_down, width_factors, unit_factors, slot_block):
+def plain(hidden_in, norm_gain, w_gate, w_up, w_down, width_factors, unit_factors, slot_block):
     n_replica = lax.axis_size("rollout")
     n_tensor = lax.axis_size("tensor")
     n = n_replica * n_tensor
@@ -52,6 +54,262 @@
     return (hidden_in.astype(f32) + mixed).astype(jnp.bfloat16)
 
 
+F32 = jnp.float32
+BF = jnp.bfloat16
+NB = 3
+KC = 512
+
+
+def kernel(inv_ref, x_ref, a_ref, b_ref, gain_ref, wg, wu, wd, o_ref,
+           xr, xs, ag, b1, b2s, bb, acc, pacc, small, psmall, wbuf, dbuf, actb, ab_ref, tb, rb,
+           x_s, x_r, a_s, a_r, b1_s, b1_r, b2_s, b2_r, one_s, one_r, t_s, t_r, w_sem, d_sem):
+    r = lax.axis_index("rollout")
+    t = lax.axis_index("tensor")
+    me = r * 8 + t
+    other = 1 - r
+    units = wg.shape[1]
+    wide = acc.shape[2]
+    shift = units // 2 % 128
+    base = units // 2 - shift
+
+    def rcopy(src, dst, ss, rs, rr, tt):
+        return pltpu.make_async_remote_copy(
+            src_ref=src, dst_ref=dst, send_sem=ss, recv_sem=rs,
+            device_id={"rollout": rr, "tensor": tt}, device_id_type=pl.DeviceIdType.MESH)
+
+    def wcopy(w, k, s):
+        slot = lax.rem(s, NB)
+        return pltpu.make_async_copy(w.at[pl.ds(k * KC, KC), :], wbuf.at[slot], w_sem.at[slot])
+
+    def dcopy(n):
+        slot = lax.rem(n, NB)
+        cols = pl.ds(pl.multiple_of(n * KC, KC), KC)
+        return pltpu.make_async_copy(wd.at[:, cols], dbuf.at[slot], d_sem.at[slot])
+
+    for s in range(NB):
+        wcopy(wg, s, jnp.int32(s)).start()
+
+    barrier = pltpu.get_barrier_semaphore()
+
+    @pl.loop(1, 16)
+    def _(o):
+        p = lax.rem(me + o, 16)
+        pl.semaphore_signal(barrier, inc=1, device_id={"rollout": p // 8, "tensor": lax.rem(p, 8)},
+                            device_id_type=pl.DeviceIdType.MESH)
+
+    pl.semaphore_wait(barrier, 15)
+
+    def x_send(p):
+        return rcopy(x_ref, xr.at[t], x_s.at[p], x_r.at[t], r, p)
+
+    def x_recv(p):
+        return rcopy(x_ref, xr.at[p], x_s.at[p], x_r.at[p], r, p)
+
+    def a_send(p):
+        return rcopy(a_ref, ag.at[t], a_s.at[p], a_r.at[t], r, p)
+
+    def a_recv(p):
+        return rcopy(a_ref, ag.at[p], a_s.at[p], a_r.at[p], r, p)
+
+    def b1_send(p):
+        return rcopy(b_ref.at[p], b1.at[me], b1_s.at[p], b1_r.at[me], p // 8, lax.rem(p, 8))
+
+    def b1_recv(p):
+        return rcopy(b_ref.at[p], b1.at[p], b1_s.at[p], b1_r.at[p], p // 8, lax.rem(p, 8))
+
+    def b2_send(p):
+        return rcopy(b2s.at[p], bb.at[p // 8, me], b2_s.at[p], b2_r.at[me], p // 8, lax.rem(p, 8))
+
+    def b2_recv(p):
+        return rcopy(b2s.at[p], bb.at[r, p], b2_s.at[p], b2_r.at[p], p // 8, lax.rem(p, 8))
+
+    def t_send(n, p):
+        return rcopy(tb.at[n, p], rb.at[n, t], t_s.at[n, p], t_r.at[n, t], r, p)
+
+    def t_recv(n, p):
+        return rcopy(tb.at[n, p], rb.at[n, p], t_s.at[n, p], t_r.at[n, p], r, p)
+
+    def peers(count, mine, fn):
+        @pl.loop(1, count)
+        def _(o):
+            fn(lax.rem(mine + o, count))
+
+    peers(8, t, lambda p: x_send(p).start())
+    peers(8, t, lambda p: a_send(p).start())
+    peers(16, me, lambda p: b1_send(p).start())
+    xr[t] = x_ref[...]
+    ag[t] = a_ref[...]
+    b1[me] = b_ref[me]
+    acc[...] = jnp.zeros_like(acc)
+    for n in range(NB):
+        dcopy(jnp.int32(n)).start()
+    peers(8, t, lambda p: x_recv(p).wait_recv())
+
+    vs = [xr[p].astype(F32) for p in range(8)]
+    sq = jnp.zeros((64, 1), F32)
+    for c in range(8):
+        h, cc = c // 4, c % 4
+        v = jnp.concatenate([vs[p][8 * h:8 * h + 8, KC * cc:KC * cc + KC] for p in range(8)], axis=0)
+        sq = sq + jnp.sum(v * v, axis=1, keepdims=True)
+        xs[c] = (v * gain_ref[c]).astype(BF)
+    small[1] = jnp.broadcast_to(sq, (64, 128))
+
+    def step(w_next, which, first):
+        @pl.loop(0, 8)
+        def _(k):
+            s = first + k
+            wcopy(wg, k, s).wait()
+            acc[which, :, 0:units] += jnp.dot(xs[k], wbuf[lax.rem(s, NB)], preferred_element_type=F32)
+
+            @pl.when(k + NB < 8)
+            def _():
+                wcopy(wg if which == 0 else wu, k + NB, s).start()
+
+            if w_next is not None:
+                @pl.when(k + NB >= 8)
+                def _():
+                    wcopy(w_next, k + NB - 8, s).start()
+
+    step(wu, 0, 0)
+    sums = [rcopy(acc.at[w], pacc.at[w], one_s.at[w], one_r.at[w], other, t) for w in range(2)]
+    sums[0].start()
+    peers(16, me, lambda p: b1_recv(p).wait_recv())
+
+    @pl.loop(1, 16)
+    def _(o):
+        p = lax.rem(me + o, 16)
+        b2s[p] = b1[inv_ref[2 * lax.rem(p, 8) + p // 8]]
+        b2_send(p).start()
+
+    bb[r, me] = b1[inv_ref[2 * t + r]]
+
+    peers(8, t, lambda p: a_recv(p).wait_recv())
+    xa = jnp.zeros((64, 128), F32)
+    for c in range(8):
+        xa = xa + lax.dot_general(xs[c], ag[c, 0:128, :], (((1,), (1,)), ((), ())), preferred_element_type=F32)
+    small[0] = xa
+    tiny = rcopy(small, psmall, one_s.at[2], one_r.at[2], other, t)
+    tiny.start()
+
+    step(None, 1, 8)
+    sums[1].start()
+    peers(16, me, lambda p: b2_recv(p).wait_recv())
+    fwd = rcopy(bb.at[r], bb.at[r], one_s.at[3], one_r.at[3], other, t)
+    fwd.start()
+    tiny.wait_recv()
+    xaf = (0.5 * (small[0] + psmall[0])).astype(BF)
+    inv_rms = lax.rsqrt((small[1, :, 0:1] + psmall[1, :, 0:1]) / D + 1e-06)
+    rcopy(bb.at[other], bb.at[other], one_s.at[3], one_r.at[3], other, t).wait_recv()
+    sums[0].wait_recv()
+    sums[1].wait_recv()
+
+    def chunk(which, b, k):
+        return jnp.concatenate([bb[which, a * 4 + b, k] for a in range(4)], axis=0)
+
+    def low(k):
+        lhs = xaf[:, 64 * k:64 * k + 64]
+        parts = [[jnp.dot(lhs, chunk(w, b, k), preferred_element_type=F32) for b in range(4)] for w in range(2)]
+        none = jnp.zeros((64, wide - 2048), F32)
+        left = jnp.concatenate(parts[0] + [none], axis=1)
+        right = jnp.concatenate([none] + parts[1], axis=1)
+        return left + pltpu.roll(right, shift, 1)
+
+    gate = (acc[0] + pacc[0] + low(0)) * inv_rms
+    upper = (acc[1] + pacc[1] + low(1)) * inv_rms
+    lane = lax.broadcasted_iota(jnp.int32, (64, wide), 1)
+    act = jnp.where(lane < units, gate / (1.0 + jnp.exp(-gate)) * upper, 0.0).astype(BF)
+    actb[...] = act
+    second = pltpu.roll(act.astype(F32), wide - shift, 1)[:, base:base + 2048].astype(BF)
+    ab = jnp.zeros((64, 64), F32)
+    for w in range(2):
+        half = act[:, 0:2048] if w == 0 else second
+        for b in range(4):
+            ab = ab + lax.dot_general(half[:, KC * b:KC * b + KC], chunk(w, b, 2), (((1,), (1,)), ((), ())),
+                                      preferred_element_type=F32)
+    ab_ref[...] = (0.5 * ab).astype(BF)
+
+    @pl.loop(0, 8)
+    def _(n):
+        dcopy(n).wait()
+        terms = jnp.dot(actb[:, 0:units], dbuf[lax.rem(n, NB)], preferred_element_type=F32)
+
+        @pl.when(n + NB < 8)
+        def _():
+            dcopy(n + NB).start()
+
+        terms = terms + jnp.dot(ab_ref[...], ag[n, 128:192, :], preferred_element_type=F32)
+        for p in range(8):
+            tb[n, p] = jnp.concatenate(
+                [terms[8 * p:8 * p + 8, 0:256], terms[8 * p:8 * p + 8, 256:512]], axis=0).astype(BF)
+        peers(8, t, lambda p: t_send(n, p).start())
+        rb[n, t] = tb[n, t]
+
+    @pl.loop(0, 8)
+    def _(n):
+        peers(8, t, lambda p: t_recv(n, p).wait_recv())
+        total = rb[n, 0].astype(F32)
+        for p in range(1, 8):
+            total = total + rb[n, p].astype(F32)
+        o_ref[n] = total
+
+    peers(8, t, lambda p: x_send(p).wait_send())
+    peers(8, t, lambda p: a_send(p).wait_send())
+    peers(16, me, lambda p: b1_send(p).wait_send())
+    peers(16, me, lambda p: b2_send(p).wait_send())
+
+    @pl.loop(0, 8)
+    def _(n):
+        peers(8, t, lambda p: t_send(n, p).wait_send())
+
+    sums[0].wait_send()
+    sums[1].wait_send()
+    tiny.wait_send()
+    fwd.wait_send()
+
+
+def on_device(hidden_in, norm_gain, w_gate, w_up, w_down, width_factors, unit_factors, slot_block):
+    n_replica = lax.axis_size("rollout")
+    n_tensor = lax.axis_size("tensor")
+    block, rank = unit_factors.shape[1:]
+    rows, half = hidden_in.shape
+    units = w_gate.shape[1]
+    fits = (n_replica, n_tensor, rank, rows, half) == (2, 8, 64, 8, 4096) and 1536 < block <= 2048
+    if not fits or units != 2 * block or units % 16:
+        return plain(hidden_in, norm_gain, w_gate, w_up, w_down, width_factors, unit_factors, slot_block)
+    wide = 128 * (units // 2 // 128) + 2048
+    inv = jnp.argmax(slot_block[None, :] == jnp.arange(16, dtype=jnp.int32)[:, None], axis=1).astype(jnp.int32)
+    x = jnp.concatenate([hidden_in[:, :2048], hidden_in[:, 2048:]], axis=0)
+    a = jnp.swapaxes(width_factors, 1, 2).reshape(192, 512)
+    b = jnp.pad(jnp.swapaxes(unit_factors, 1, 2), ((0, 0), (0, 0), (0, 2048 - block)))
+    b = b.reshape(3, 4, 16, 4, 512).transpose(1, 3, 0, 2, 4).reshape(16, 3, 16, 512)
+    gain = norm_gain.reshape(8, 1, 512)
+    vmem = pl.BlockSpec(memory_space=pltpu.VMEM)
+    hbm = pl.BlockSpec(memory_space=pltpu.HBM)
+    dma = pltpu.SemaphoreType.DMA
+    out = pl.pallas_call(
+        kernel,
+        out_shape=jax.ShapeDtypeStruct((8, 16, 256), F32),
+        in_specs=[pl.BlockSpec(memory_space=pltpu.SMEM), vmem, vmem, vmem, vmem, hbm, hbm, hbm],
+        out_specs=vmem,
+        scratch_shapes=[
+            pltpu.VMEM((8, 16, 2048), BF), pltpu.VMEM((8, 64, 512), BF), pltpu.VMEM((8, 192, 512), BF),
+            pltpu.VMEM((16, 3, 16, 512), BF), pltpu.VMEM((16, 3, 16, 512), BF), pltpu.VMEM((2, 16, 3, 16, 512), BF),
+            pltpu.VMEM((2, 64, wide), F32), pltpu.VMEM((2, 64, wide), F32),
+            pltpu.VMEM((2, 64, 128), F32), pltpu.VMEM((2, 64, 128), F32),
+            pltpu.VMEM((NB, KC, units), BF), pltpu.VMEM((NB, units, KC), BF),
+            pltpu.VMEM((64, wide), BF), pltpu.VMEM((64, 64), BF),
+            pltpu.VMEM((8, 8, 16, 256), BF), pltpu.VMEM((8, 8, 16, 256), BF),
+            dma((8,)), dma((8,)), dma((8,)), dma((8,)), dma((16,)), dma((16,)), dma((16,)), dma((16,)),
+            dma((4,)), dma((4,)), dma((8, 8)), dma((8, 8)), dma((NB,)), dma((NB,)),
+        ],
+        compiler_params=pltpu.CompilerParams(collective_id=0, has_side_effects=True,
+                                             vmem_limit_bytes=56 * 1024 * 1024),
+        cost_estimate=pl.CostEstimate(flops=11_600_000_000, bytes_accessed=92_000_000, transcendentals=240_000),
+    )(inv, x, a, b, gain, w_gate, w_up, w_down)
+    mixed = out.reshape(8, 2, 8, 256).transpose(2, 0, 1, 3).reshape(8, 4096)
+    return (hidden_in.astype(F32) + mixed).astype(BF)
+
+
 def solution(mesh):
     in_specs = (
         P(("groups", "tensor"), "rollout"),

time: 255 us -> 192 us (0.75)
  Pallas kernels: 0 us -> 110 us
  waiting for transfers between devices: 106 us -> 0 us
  local copies, waits for them, and re-layouts: 8.12 us -> 76.6 us
  blocking collectives: 62.7 us -> 0 us
  matrix products: 52.4 us -> 0 us
  between operations: 13.2 us -> 0.04 us
  starting transfers between devices: 7.55 us -> 0 us
    pallas_call x0 -> x1, Pallas kernels: none -> 110 us  [on_device(): pl.pallas_call(kernel, out_shape=jax.ShapeDtypeStruct((8, 16, 256), F32),...]
    unnamed x9 -> x4, local copies, waits for them, and re-layouts: 1.07 us -> 72.9 us
    reduce_scatter x1 -> x0, waiting for transfers between devices: 65.1 us -> none  [on_device(): mixed = lax.psum_scatter(terms, 'tensor', scatter_dimension=0, tiled=True)]
    dot_general x6 -> x0, matrix products: 52.4 us -> none  [the longest x1 15.6 us: on_device(): gate = jnp.dot(scaled, w_gate, preferred_element_type=f32)]
    all_gather x1 -> x0, blocking collectives: 31.8 us -> none  [on_device(): rows = lax.all_gather(hidden_in, 'tensor', axis=0, tiled=True)]
    all_to_all x1 -> x0, blocking collectives: 28.3 us -> none  [on_device(): own = lax.all_to_all(sorted_, ('rollout', 'tensor'), 0, 0, tiled=True)]
    all_to_all x1 -> x0, waiting for transfers between devices: 24.3 us -> none  [on_device(): every = lax.all_to_all(flat, ('rollout', 'tensor'), 0, 0, tiled=True)]
    psum x1 -> x0, waiting for transfers between devices: 15.9 us -> none  [on_device(): upper = lax.psum(upper, 'rollout')]
  transfers between devices with their start and end apart: 5 -> 0, of which waited for: 3 -> 0; matrix products, arithmetic and copies ran while one was open for 14% -> 0% of each run, Pallas kernels for 0% -> 0%
where the time goes in v2:
time: 192 us; the launch traced here: 190 us
  Pallas kernels  110 us (57%)
  local copies, waits for them, and re-layouts  76.6 us (40%)
  other arithmetic  3.5 us (2%)
    pallas_call x1, Pallas kernels, on_device(): pl.pallas_call(kernel, out_shape=jax.ShapeDtypeStruct((8, 16, 256), F32),...  110 us
    unnamed x4, local copies, waits for them, and re-layouts  72.9 us

profile of v2, /device:TPU:0, one launch (start us, length us, event | category | flops | bytes accessed | tf_op | source)
XLA Modules:
  0.0 189.8 jit_solution(15228498081121218903)
XLA Ops:
  0.0 1.3 iota_reduce_fusion
  1.3 0.8 fusion
  2.1 0.6 pad_maximum_fusion.x_ref
  2.7 1.2 pad.4
  4.0 0.6 reshape.20
  4.5 1.1 copy.12
  5.6 36.6 %copy.13.wg = bf16[4096,3696]{1,0:T(8,128)(2,1)} copy(bf16[4096,3696]{0,1:T(8,128)(2,1)} %param.10) | data formatting | bytes 60555264 | tf_op args[2]
  42.2 36.4 %copy.14.wu = bf16[4096,3696]{1,0:T(8,128)(2,1)} copy(bf16[4096,3696]{0,1:T(8,128)(2,1)} %param.11) | data formatting | bytes 60555264 | tf_op args[3]
  78.5 0.0 copy-start
  78.5 109.7 %shard_map.82 = f32[8,16,256]{2,1,0:T(8,128)} custom-call(s32[16]{0:T(128)} %get-tuple-element.6.inv_ref, bf16[16,2048]{1,0:T(8,128)(2,1)} %pad_maximum_fusion.x_ref, bf16[192,512]{1,0:T(8,128)(2,1)} %bitcast.16, bf16[16,3,16,512]{3,2,1,0:T(8,128)(2,1)} %bitcast.13, f32[8,1,512]{2,1,0:T(1,128)} %bitcast.17, bf16[4096,3696]{1,0:T(8,128)(2,1)} %copy.13.wg, ...), custom_call_target="tpu_custom_call" | custom-call | flops 11600000000 | bytes 92000000 | tf_op jit(solution)/shard_map/pallas_call | solution.py:289
  188.2 0.0 copy-done
  188.2 1.5 add_convert_fusion
Async XLA Ops:
  78.5 109.7 %copy-start = (bf16[8,4096]{1,0:T(8,128)(2,1)S(1)}, bf16[8,4096]{1,0:T(8,128)(2,1)}, u32[]{:S(2)}) copy-start(bf16[8,4096]{1,0:T(8,128)(2,1)} %param.8) | copy-start | bytes 196612

commit v3 on v2

--- a/solution.py
+++ b/solution.py
@@ -56,18 +56,19 @@
 
 F32 = jnp.float32
 BF = jnp.bfloat16
-NB = 3
+NB = 6
 KC = 512
 
 
 def kernel(inv_ref, x_ref, a_ref, b_ref, gain_ref, wg, wu, wd, o_ref,
-           xr, xs, ag, b1, b2s, bb, acc, pacc, small, psmall, wbuf, dbuf, actb, ab_ref, tb, rb,
-           x_s, x_r, a_s, a_r, b1_s, b1_r, b2_s, b2_r, one_s, one_r, t_s, t_r, w_sem, d_sem):
+           xr, xs, pa, pb, b1, b2s, bb, acc, pacc, small, psmall, wbuf, actb, tb, rb,
+           x_s, x_r, a_s, a_r, c_s, c_r, f_s, f_r, b1_s, b1_r, b2_s, b2_r, one_s, one_r, t_s, t_r, w_sem):
     r = lax.axis_index("rollout")
     t = lax.axis_index("tensor")
     me = r * 8 + t
     other = 1 - r
-    units = wg.shape[1]
+    beside = t + 1 - 2 * lax.rem(t, 2)
+    units = wg.shape[0]
     wide = acc.shape[2]
     shift = units // 2 % 128
     base = units // 2 - shift
@@ -79,15 +80,17 @@
 
     def wcopy(w, k, s):
         slot = lax.rem(s, NB)
-        return pltpu.make_async_copy(w.at[pl.ds(k * KC, KC), :], wbuf.at[slot], w_sem.at[slot])
-
-    def dcopy(n):
-        slot = lax.rem(n, NB)
-        cols = pl.ds(pl.multiple_of(n * KC, KC), KC)
-        return pltpu.make_async_copy(wd.at[:, cols], dbuf.at[slot], d_sem.at[slot])
+        cols = pl.ds(pl.multiple_of(k * KC, KC), KC)
+        return pltpu.make_async_copy(w.at[:, cols], wbuf.at[slot], w_sem.at[slot])
+
+    def prefetch(s):
+        for i, w in enumerate((wg, wu, wd)):
+            @pl.when((s >= 8 * i) & (s < 8 * i + 8))
+            def _():
+                wcopy(w, s - 8 * i, s).start()
 
     for s in range(NB):
-        wcopy(wg, s, jnp.int32(s)).start()
+        wcopy(wg, jnp.int32(s), jnp.int32(s)).start()
 
     barrier = pltpu.get_barrier_semaphore()
 
@@ -102,14 +105,29 @@
     def x_send(p):
         return rcopy(x_ref, xr.at[t], x_s.at[p], x_r.at[t], r, p)
 
+    def x_pass(p):
+        return rcopy(xr.at[p], xr.at[p], f_s.at[p], x_r.at[p], r, beside)
+
     def x_recv(p):
         return rcopy(x_ref, xr.at[p], x_s.at[p], x_r.at[p], r, p)
 
     def a_send(p):
-        return rcopy(a_ref, ag.at[t], a_s.at[p], a_r.at[t], r, p)
+        return rcopy(pa.at[t], pa.at[t], a_s.at[p], a_r.at[t], r, p)
 
     def a_recv(p):
-        return rcopy(a_ref, ag.at[p], a_s.at[p], a_r.at[p], r, p)
+        return rcopy(pa.at[p], pa.at[p], a_s.at[p], a_r.at[p], r, p)
+
+    def c_send(p):
+        return rcopy(pb.at[t], pb.at[t], c_s.at[p], c_r.at[t], r, p)
+
+    def c_recv(p):
+        return rcopy(pb.at[p], pb.at[p], c_s.at[p], c_r.at[p], r, p)
+
+    def f_send(p):
+        return rcopy(bb.at[r, p], bb.at[r, p], f_s.at[8 + p], f_r.at[p], other, t)
+
+    def f_recv(p):
+        return rcopy(bb.at[other, p], bb.at[other, p], f_s.at[8 + p], f_r.at[p], other, t)
 
     def b1_send(p):
         return rcopy(b_ref.at[p], b1.at[me], b1_s.at[p], b1_r.at[me], p // 8, lax.rem(p, 8))
@@ -134,16 +152,20 @@
         def _(o):
             fn(lax.rem(mine + o, count))
 
-    peers(8, t, lambda p: x_send(p).start())
-    peers(8, t, lambda p: a_send(p).start())
-    peers(16, me, lambda p: b1_send(p).start())
+    column = [lax.rem(t + 2 * o, 8) for o in (1, 3, 2)]
+    for p in column:
+        x_send(p).start()
+    x_send(beside).start()
     xr[t] = x_ref[...]
-    ag[t] = a_ref[...]
     b1[me] = b_ref[me]
     acc[...] = jnp.zeros_like(acc)
-    for n in range(NB):
-        dcopy(jnp.int32(n)).start()
-    peers(8, t, lambda p: x_recv(p).wait_recv())
+    for p in column:
+        x_recv(p).wait_recv()
+        x_pass(p).start()
+    x_recv(beside).wait_recv()
+    for p in column:
+        x_recv(p + beside - t).wait_recv()
+    peers(16, me, lambda p: b1_send(p).start())
 
     vs = [xr[p].astype(F32) for p in range(8)]
     sq = jnp.zeros((64, 1), F32)
@@ -154,23 +176,20 @@
         xs[c] = (v * gain_ref[c]).astype(BF)
     small[1] = jnp.broadcast_to(sq, (64, 128))
 
-    def step(w_next, which, first):
+    pa[t] = lax.dot_general(xs[t], a_ref[0:128, :], (((1,), (1,)), ((), ())),
+                            preferred_element_type=F32).astype(BF)
+    peers(8, t, lambda p: a_send(p).start())
+
+    def step(which):
         @pl.loop(0, 8)
         def _(k):
-            s = first + k
+            s = 8 * which + k
             wcopy(wg, k, s).wait()
-            acc[which, :, 0:units] += jnp.dot(xs[k], wbuf[lax.rem(s, NB)], preferred_element_type=F32)
-
-            @pl.when(k + NB < 8)
-            def _():
-                wcopy(wg if which == 0 else wu, k + NB, s).start()
-
-            if w_next is not None:
-                @pl.when(k + NB >= 8)
-                def _():
-                    wcopy(w_next, k + NB - 8, s).start()
-
-    step(wu, 0, 0)
+            acc[which, :, 0:units] += lax.dot_general(
+                xs[k], wbuf[lax.rem(s, NB)], (((1,), (1,)), ((), ())), preferred_element_type=F32)
+            prefetch(s + NB)
+
+    step(0)
     sums = [rcopy(acc.at[w], pacc.at[w], one_s.at[w], one_r.at[w], other, t) for w in range(2)]
     sums[0].start()
     peers(16, me, lambda p: b1_recv(p).wait_recv())
@@ -184,22 +203,30 @@
     bb[r, me] = b1[inv_ref[2 * t + r]]
 
     peers(8, t, lambda p: a_recv(p).wait_recv())
-    xa = jnp.zeros((64, 128), F32)
-    for c in range(8):
-        xa = xa + lax.dot_general(xs[c], ag[c, 0:128, :], (((1,), (1,)), ((), ())), preferred_element_type=F32)
+    xa = pa[0].astype(F32)
+    for p in range(1, 8):
+        xa = xa + pa[p].astype(F32)
     small[0] = xa
     tiny = rcopy(small, psmall, one_s.at[2], one_r.at[2], other, t)
     tiny.start()
 
-    step(None, 1, 8)
+    step(1)
     sums[1].start()
-    peers(16, me, lambda p: b2_recv(p).wait_recv())
-    fwd = rcopy(bb.at[r], bb.at[r], one_s.at[3], one_r.at[3], other, t)
-    fwd.start()
+    f_send(me).start()
+
+    def onward(p):
+        b2_recv(p).wait_recv()
+        f_send(p).start()
+
+    peers(16, me, onward)
     tiny.wait_recv()
     xaf = (0.5 * (small[0] + psmall[0])).astype(BF)
     inv_rms = lax.rsqrt((small[1, :, 0:1] + psmall[1, :, 0:1]) / D + 1e-06)
-    rcopy(bb.at[other], bb.at[other], one_s.at[3], one_r.at[3], other, t).wait_recv()
+
+    @pl.loop(0, 16)
+    def _(p):
+        f_recv(p).wait_recv()
+
     sums[0].wait_recv()
     sums[1].wait_recv()
 
@@ -226,23 +253,33 @@
         for b in range(4):
             ab = ab + lax.dot_general(half[:, KC * b:KC * b + KC], chunk(w, b, 2), (((1,), (1,)), ((), ())),
                                       preferred_element_type=F32)
-    ab_ref[...] = (0.5 * ab).astype(BF)
-
-    @pl.loop(0, 8)
-    def _(n):
-        dcopy(n).wait()
-        terms = jnp.dot(actb[:, 0:units], dbuf[lax.rem(n, NB)], preferred_element_type=F32)
-
-        @pl.when(n + NB < 8)
-        def _():
-            dcopy(n + NB).start()
-
-        terms = terms + jnp.dot(ab_ref[...], ag[n, 128:192, :], preferred_element_type=F32)
+    pb[t] = jnp.concatenate([0.5 * ab, jnp.zeros((64, 64), F32)], axis=1).astype(BF)
+    peers(8, t, lambda p: c_send(p).start())
+
+    def hand_on(n, terms):
         for p in range(8):
             tb[n, p] = jnp.concatenate(
                 [terms[8 * p:8 * p + 8, 0:256], terms[8 * p:8 * p + 8, 256:512]], axis=0).astype(BF)
         peers(8, t, lambda p: t_send(n, p).start())
         rb[n, t] = tb[n, t]
+
+    @pl.loop(0, 8)
+    def _(n):
+        s = 16 + n
+        wcopy(wd, n, s).wait()
+        terms = jnp.dot(actb[:, 0:units], wbuf[lax.rem(s, NB)], preferred_element_type=F32)
+        prefetch(s + NB)
+        hand_on(n, terms)
+
+        @pl.when(n == 3)
+        def _():
+            peers(8, t, lambda p: c_recv(p).wait_recv())
+            whole = pb[0].astype(F32)
+            for p in range(1, 8):
+                whole = whole + pb[p].astype(F32)
+            hand_on(8, jnp.dot(whole[:, 0:64].astype(BF), a_ref[128:192, :], preferred_element_type=F32))
+
+    peers(8, t, lambda p: t_recv(8, p).wait_recv())
 
     @pl.loop(0, 8)
     def _(n):
@@ -250,21 +287,28 @@
         total = rb[n, 0].astype(F32)
         for p in range(1, 8):
             total = total + rb[n, p].astype(F32)
-        o_ref[n] = total
-
-    peers(8, t, lambda p: x_send(p).wait_send())
+        o_ref[n] = total + rb[8, n].astype(F32)
+
+    for p in column:
+        x_send(p).wait_send()
+        x_pass(p).wait_send()
+    x_send(beside).wait_send()
+    peers(8, t, lambda p: c_send(p).wait_send())
     peers(8, t, lambda p: a_send(p).wait_send())
     peers(16, me, lambda p: b1_send(p).wait_send())
     peers(16, me, lambda p: b2_send(p).wait_send())
 
-    @pl.loop(0, 8)
+    @pl.loop(0, 9)
     def _(n):
         peers(8, t, lambda p: t_send(n, p).wait_send())
+
+    @pl.loop(0, 16)
+    def _(p):
+        f_send(p).wait_send()
 
     sums[0].wait_send()
     sums[1].wait_send()
     tiny.wait_send()
-    fwd.wait_send()
 
 
 def on_device(hidden_in, norm_gain, w_gate, w_up, w_down, width_factors, unit_factors, slot_block):
@@ -292,20 +336,21 @@
         in_specs=[pl.BlockSpec(memory_space=pltpu.SMEM), vmem, vmem, vmem, vmem, hbm, hbm, hbm],
         out_specs=vmem,
         scratch_shapes=[
-            pltpu.VMEM((8, 16, 2048), BF), pltpu.VMEM((8, 64, 512), BF), pltpu.VMEM((8, 192, 512), BF),
+            pltpu.VMEM((8, 16, 2048), BF), pltpu.VMEM((8, 64, 512), BF), pltpu.VMEM((8, 64, 128), BF), pltpu.VMEM((8, 64, 128), BF),
             pltpu.VMEM((16, 3, 16, 512), BF), pltpu.VMEM((16, 3, 16, 512), BF), pltpu.VMEM((2, 16, 3, 16, 512), BF),
             pltpu.VMEM((2, 64, wide), F32), pltpu.VMEM((2, 64, wide), F32),
             pltpu.VMEM((2, 64, 128), F32), pltpu.VMEM((2, 64, 128), F32),
-            pltpu.VMEM((NB, KC, units), BF), pltpu.VMEM((NB, units, KC), BF),
-            pltpu.VMEM((64, wide), BF), pltpu.VMEM((64, 64), BF),
-            pltpu.VMEM((8, 8, 16, 256), BF), pltpu.VMEM((8, 8, 16, 256), BF),
-            dma((8,)), dma((8,)), dma((8,)), dma((8,)), dma((16,)), dma((16,)), dma((16,)), dma((16,)),
-            dma((4,)), dma((4,)), dma((8, 8)), dma((8, 8)), dma((NB,)), dma((NB,)),
+            pltpu.VMEM((NB, units, KC), BF),
+            pltpu.VMEM((64, wide), BF),
+            pltpu.VMEM((9, 8, 16, 256), BF), pltpu.VMEM((9, 8, 16, 256), BF),
+            dma((8,)), dma((8,)), dma((8,)), dma((8,)), dma((8,)), dma((8,)), dma((24,)), dma((16,)),
+            dma((16,)), dma((16,)), dma((16,)), dma((16,)),
+            dma((3,)), dma((3,)), dma((9, 8)), dma((9, 8)), dma((NB,)),
         ],
         compiler_params=pltpu.CompilerParams(collective_id=0, has_side_effects=True,
                                              vmem_limit_bytes=56 * 1024 * 1024),
         cost_estimate=pl.CostEstimate(flops=11_600_000_000, bytes_accessed=92_000_000, transcendentals=240_000),
-    )(inv, x, a, b, gain, w_gate, w_up, w_down)
+    )(inv, x, a, b, gain, w_gate.T, w_up.T, w_down)
     mixed = out.reshape(8, 2, 8, 256).transpose(2, 0, 1, 3).reshape(8, 4096)
     return (hidden_in.astype(F32) + mixed).astype(BF)
 

time: 192 us -> 86.2 us (0.45)
  local copies, waits for them, and re-layouts: 76.6 us -> 3.61 us
  Pallas kernels: 110 us -> 78.7 us
    unnamed x4 -> x2, local copies, waits for them, and re-layouts: 72.9 us -> 0.01 us
    pallas_call x1, Pallas kernels: 110 us -> 78.7 us  [on_device(): pl.pallas_call(kernel, out_shape=jax.ShapeDtypeStruct((8, 16, 256), F32),...]
where the time goes in v3:
time: 86.2 us; the launch traced here: 85.9 us
  Pallas kernels  78.7 us (91%)
  local copies, waits for them, and re-layouts  3.61 us (4%)
  other arithmetic  3.53 us (4%)
    pallas_call x1, Pallas kernels, on_device(): pl.pallas_call(kernel, out_shape=jax.ShapeDtypeStruct((8, 16, 256), F32),...  78.7 us

profile of v3, /device:TPU:0, one launch (start us, length us, event | category | flops | bytes accessed | tf_op | source)
XLA Modules:
  0.0 85.9 jit_solution(11519316121734770244)
XLA Ops:
  0.0 0.8 fusion
  0.8 0.6 pad_maximum_fusion.x_ref
  1.4 1.2 %pad.4 = bf16[3,64,2048]{2,1,0:T(8,128)(2,1)S(1)} pad(bf16[3,64,1848]{2,1,0:T(8,128)(2,1)} %bitcast.18, bf16[]{:T(256)} %constant.8.clone.1), padding=0_0x0_0x0_200 | pad | bytes 1496066 | tf_op jit(solution)/shard_map/jit(_pad)/pad | solution.py:327
  2.6 0.6 reshape.20
  3.2 1.0 %copy.10 = bf16[3,4,16,4,512]{4,2,0,3,1:T(8,128)(2,1)} copy(bf16[3,4,16,4,512]{4,3,2,1,0:T(4,128)(2,1)S(1)} %reshape.20) | data formatting | bytes 1572864 | tf_op jit(solution)/shard_map/reshape | solution.py:328
  4.3 1.4 %iota_reduce_fusion = (pred[16]{0:T(512)(128)(4,1)}, s32[16]{0:T(128)}) fusion(s32[16]{0:T(128)} %param.15), kind=kLoop, calls=%fused_computation.2 | loop fusion | flops 1936 | bytes 144 | tf_op jit(solution)/shard_map/on_device/reduce | solution.py:324
  5.6 0.0 copy-start
  5.6 78.7 %shard_map.82 = f32[8,16,256]{2,1,0:T(8,128)} custom-call(s32[16]{0:T(128)} %get-tuple-element.6.inv_ref, bf16[16,2048]{1,0:T(8,128)(2,1)} %pad_maximum_fusion.x_ref, bf16[192,512]{1,0:T(8,128)(2,1)} %bitcast.20, bf16[16,3,16,512]{3,2,1,0:T(8,128)(2,1)} %bitcast.17, f32[8,1,512]{2,1,0:T(1,128)} %bitcast.21, bf16[3696,4096]{1,0:T(8,128)(2,1)} %bitcast.15, ...), custom_call_target="tpu_custom_call" | custom-call | flops 11600000000 | bytes 92000000 | tf_op jit(solution)/shard_map/pallas_call | solution.py:333
  84.3 0.0 copy-done
  84.3 1.5 %add_convert_fusion = bf16[8,4096]{1,0:T(8,128)(2,1)} fusion(f32[8,4096]{1,0:T(8,128)} %bitcast.19, bf16[8,4096]{1,0:T(8,128)(2,1)S(1)} %copy-done), kind=kLoop, calls=%fused_computation | loop fusion | flops 98304 | bytes 262144 | tf_op jit(solution)/shard_map/convert_element_type | solution.py:355
Async XLA Ops:
  5.6 78.7 %copy-start = (bf16[8,4096]{1,0:T(8,128)(2,1)S(1)}, bf16[8,4096]{1,0:T(8,128)(2,1)}, u32[]{:S(2)}) copy-start(bf16[8,4096]{1,0:T(8,128)(2,1)} %param.8) | copy-start | bytes 196612

commit v4 on v3

--- a/solution.py
+++ b/solution.py
@@ -156,6 +156,7 @@
     for p in column:
         x_send(p).start()
     x_send(beside).start()
+    peers(16, me, lambda p: b1_send(p).start())
     xr[t] = x_ref[...]
     b1[me] = b_ref[me]
     acc[...] = jnp.zeros_like(acc)
@@ -165,7 +166,6 @@
     x_recv(beside).wait_recv()
     for p in column:
         x_recv(p + beside - t).wait_recv()
-    peers(16, me, lambda p: b1_send(p).start())
 
     vs = [xr[p].astype(F32) for p in range(8)]
     sq = jnp.zeros((64, 1), F32)

time: 86.2 us -> 82.4 us (0.956)
  Pallas kernels: 78.7 us -> 74.9 us
    pallas_call x1, Pallas kernels: 78.7 us -> 74.9 us  [on_device(): pl.pallas_call(kernel, out_shape=jax.ShapeDtypeStruct((8, 16, 256), F32),...]
where the time goes in v4:
time: 82.4 us; the launch traced here: 82.1 us
  Pallas kernels  74.9 us (91%)
  local copies, waits for them, and re-layouts  3.61 us (4%)
  other arithmetic  3.53 us (4%)
    pallas_call x1, Pallas kernels, on_device(): pl.pallas_call(kernel, out_shape=jax.ShapeDtypeStruct((8, 16, 256), F32),...  74.9 us

profile of v4, /device:TPU:0, one launch (start us, length us, event | category | flops | bytes accessed | tf_op | source)
XLA Modules:
  0.0 82.1 jit_solution(17894139999402868170)
XLA Ops:
  0.0 0.8 fusion
  0.8 0.6 pad_maximum_fusion.x_ref
  1.4 1.2 %pad.4 = bf16[3,64,2048]{2,1,0:T(8,128)(2,1)S(1)} pad(bf16[3,64,1848]{2,1,0:T(8,128)(2,1)} %bitcast.18, bf16[]{:T(256)} %constant.8.clone.1), padding=0_0x0_0x0_200 | pad | bytes 1496066 | tf_op jit(solution)/shard_map/jit(_pad)/pad | solution.py:327
  2.6 0.6 reshape.20
  3.2 1.0 %copy.10 = bf16[3,4,16,4,512]{4,2,0,3,1:T(8,128)(2,1)} copy(bf16[3,4,16,4,512]{4,3,2,1,0:T(4,128)(2,1)S(1)} %reshape.20) | data formatting | bytes 1572864 | tf_op jit(solution)/shard_map/reshape | solution.py:328
  4.3 1.4 %iota_reduce_fusion = (pred[16]{0:T(512)(128)(4,1)}, s32[16]{0:T(128)}) fusion(s32[16]{0:T(128)} %param.15), kind=kLoop, calls=%fused_computation.2 | loop fusion | flops 1936 | bytes 144 | tf_op jit(solution)/shard_map/on_device/reduce | solution.py:324
  5.6 0.0 copy-start
  5.6 74.9 %shard_map.82 = f32[8,16,256]{2,1,0:T(8,128)} custom-call(s32[16]{0:T(128)} %get-tuple-element.6.inv_ref, bf16[16,2048]{1,0:T(8,128)(2,1)} %pad_maximum_fusion.x_ref, bf16[192,512]{1,0:T(8,128)(2,1)} %bitcast.20, bf16[16,3,16,512]{3,2,1,0:T(8,128)(2,1)} %bitcast.17, f32[8,1,512]{2,1,0:T(1,128)} %bitcast.21, bf16[3696,4096]{1,0:T(8,128)(2,1)} %bitcast.15, ...), custom_call_target="tpu_custom_call" | custom-call | flops 11600000000 | bytes 92000000 | tf_op jit(solution)/shard_map/pallas_call | solution.py:333
  80.6 0.0 copy-done
  80.6 1.5 %add_convert_fusion = bf16[8,4096]{1,0:T(8,128)(2,1)} fusion(f32[8,4096]{1,0:T(8,128)} %bitcast.19, bf16[8,4096]{1,0:T(8,128)(2,1)S(1)} %copy-done), kind=kLoop, calls=%fused_computation | loop fusion | flops 98304 | bytes 262144 | tf_op jit(solution)/shard_map/convert_element_type | solution.py:355
Async XLA Ops:
  5.6 74.9 %copy-start = (bf16[8,4096]{1,0:T(8,128)(2,1)S(1)}, bf16[8,4096]{1,0:T(8,128)(2,1)}, u32[]{:S(2)}) copy-start(bf16[8,4096]{1,0:T(8,128)(2,1)} %param.8) | copy-start | bytes 196612
